TPU v7x, 128 devices: a whole 4x4x4 slice. The times are simulated.
128 devices in a mesh: rep: 8 (over x, core), shard: 16 (over z, y).
Axes of the slice: x: 4, y: 4, z: 4, core: 2. Of those that a mesh axis runs over, the one named last changes fastest.
Arguments:
- inputs: bfloat16 [32768, 960], P(('rep', 'shard')), may hold values from -6 to 6
- seg_ids: int32 [32768], P(('rep', 'shard')), may hold values from 0 to 32767, as said below
- cotangent: bfloat16 [32768, 960], P(('rep', 'shard')), may hold values from -6 to 6
- w_query: bfloat16 [960, 960], P('shard'), may hold values from -0.1613743 to 0.1613743
- w_key: bfloat16 [960, 320], P('shard'), may hold values from -0.1613743 to 0.1613743
- w_value: bfloat16 [960, 320], P('shard'), may hold values from -0.1875 to 0.1875
- w_output: bfloat16 [960, 960], P('shard'), may hold values from -0.5 to 0.5
- w_gate: bfloat16 [960, 2560], P('shard'), may hold values from -0.1875 to 0.1875
- w_up: bfloat16 [960, 2560], P('shard'), may hold values from -0.1875 to 0.1875
- w_down: bfloat16 [2560, 960], P('shard'), may hold values from -0.125 to 0.125
- gain_attn: float32 [960], P('shard'), may hold values from 0.5 to 1.5
- gain_ffn: float32 [960], P('shard'), may hold values from 0.1 to 1.9
Outputs:
- outputs: bfloat16 [32768, 960], P(('rep', 'shard'))
- grad_inputs: bfloat16 [32768, 960], P(('rep', 'shard'))
- grad_query: float32 [960, 960], P('shard')
- grad_key: float32 [960, 320], P('shard')
- grad_value: float32 [960, 320], P('shard')
- grad_output: float32 [960, 960], P('shard')
- grad_gate: float32 [960, 2560], P('shard')
- grad_up: float32 [960, 2560], P('shard')
- grad_down: float32 [2560, 960], P('shard')
- grad_gain_attn: float32 [960], P('shard')
- grad_gain_ffn: float32 [960], P('shard')
Inputs may be any that keep to these rules, and one draw needn't show every extreme that they name: `seg_ids`: ids never fall within one device's 256 slots, each device's slots begin a new sequence, and no id is found on two devices; in every draw one device holds a single sequence of 256 tokens.
All inputs are finite; a program needn't handle non-finite values.
Results may differ from a plain program's by a relative error of at most 0.04.
Values may be sent and summed in bfloat16 or wider, within the bound.
No kernel may reach another device: no remote copies, remote signals or barrier semaphores. Data moves between devices by JAX's collectives and lax.ppermute only.
A program may use at most 128 MiB of HBM per device.

v0:
```python
import jax
import jax.numpy as jnp
from jax import lax
from jax.sharding import PartitionSpec as P

H = 15
KVH = 5


EPSILON = 1e-05
THETA = 100000.0


def mult(form, left, right):
    return jnp.einsum(form, left, right, preferred_element_type=jnp.float32)


def rms_forward(values, gain):
    scale = lax.rsqrt(jnp.mean(values * values, axis=-1, keepdims=True) + EPSILON)
    normed = values * scale
    return (normed, scale, (normed * gain).astype(jnp.bfloat16))


def rms_backward(grad_out, normed, scale, gain):
    grad_norm = grad_out * gain
    grad_in = scale * (grad_norm - normed * jnp.mean(grad_norm * normed, axis=-1, keepdims=True))
    return (grad_in, jnp.sum(grad_out * normed, axis=0))


def rotary_tables(segments, head_dim):
    count = segments.shape[-1]
    index = jnp.arange(count, dtype=jnp.int32)
    same = segments[:, :, None] == segments[:, None, :]
    first = jnp.min(jnp.where(same, index, count), axis=-1)
    position = (index - first).astype(jnp.float32)
    half = head_dim // 2
    freq = THETA ** (-jnp.arange(half, dtype=jnp.float32) / half)
    angle = position[..., None] * freq
    return (jnp.cos(angle), jnp.sin(angle))


def rotate(values, cos_table, sin_table):
    half = values.shape[-1] // 2
    first, second = (values[..., :half], values[..., half:])
    cos_part = cos_table[:, :, None, :]
    sin_part = sin_table[:, :, None, :]
    return jnp.concatenate(
        [first * cos_part - second * sin_part, second * cos_part + first * sin_part], axis=-1
    )


def unrotate(values, cos_table, sin_table):
    half = values.shape[-1] // 2
    first, second = (values[..., :half], values[..., half:])
    cos_part = cos_table[:, :, None, :]
    sin_part = sin_table[:, :, None, :]
    return jnp.concatenate(
        [first * cos_part + second * sin_part, second * cos_part - first * sin_part], axis=-1
    )


def attention_probs(query_rot, key_rot, allowed, log_total):
    scores = mult("bqkgd,btkd->bkgqt", query_rot, key_rot) * 0.125
    return jnp.where(allowed, jnp.exp(scores - log_total), 0.0)


def forward(inputs, segments, weights, heads, kv_heads):
    w_query, w_key, w_value, w_output, w_gate, w_up, w_down, gain_attn, gain_ffn = weights
    batch, count = segments.shape
    rows = inputs.shape[0]
    head_dim = w_query.shape[1] // heads
    group = heads // kv_heads
    xfloat = inputs.astype(jnp.float32)
    normed_one, scale_one, hidden_one = rms_forward(xfloat, gain_attn)
    cos_table, sin_table = rotary_tables(segments, head_dim)
    query = jnp.dot(hidden_one, w_query, preferred_element_type=jnp.float32).reshape(
        batch, count, heads, head_dim
    )
    keys = jnp.dot(hidden_one, w_key, preferred_element_type=jnp.float32).reshape(
        batch, count, kv_heads, head_dim
    )
    values = jnp.dot(hidden_one, w_value, preferred_element_type=jnp.float32).astype(jnp.bfloat16)
    values = values.reshape(batch, count, kv_heads, head_dim)
    query_rot = (
        rotate(query, cos_table, sin_table)
        .astype(jnp.bfloat16)
        .reshape(batch, count, kv_heads, group, head_dim)
    )
    key_rot = rotate(keys, cos_table, sin_table).astype(jnp.bfloat16)
    index = jnp.arange(count, dtype=jnp.int32)
    allowed = (segments[:, :, None] == segments[:, None, :]) & (index[:, None] >= index[None, :])
    allowed = allowed[:, None, None]
    scores = mult("bqkgd,btkd->bkgqt", query_rot, key_rot) * 0.125
    row_max = jnp.max(jnp.where(allowed, scores, -1e30), axis=-1, keepdims=True)
    log_total = row_max + jnp.log(
        jnp.sum(jnp.where(allowed, jnp.exp(scores - row_max), 0.0), axis=-1, keepdims=True)
    )
    probs = jnp.where(allowed, jnp.exp(scores - log_total), 0.0)
    probs_low = probs.astype(jnp.bfloat16)
    attended = (
        mult("bkgqt,btkd->bqkgd", probs_low, values)
        .astype(jnp.bfloat16)
        .reshape(rows, heads * head_dim)
    )
    mixed = xfloat + jnp.dot(attended, w_output, preferred_element_type=jnp.float32)
    normed_two, scale_two, hidden_two = rms_forward(mixed, gain_ffn)
    gate = jnp.dot(hidden_two, w_gate, preferred_element_type=jnp.float32)
    up_proj = jnp.dot(hidden_two, w_up, preferred_element_type=jnp.float32)
    sigmoid_gate = jax.nn.sigmoid(gate)
    activ = (gate * sigmoid_gate * up_proj).astype(jnp.bfloat16)
    result = (mixed + jnp.dot(activ, w_down, preferred_element_type=jnp.float32)).astype(
        jnp.bfloat16
    )
    saved = {
        "normed_one": normed_one,
        "scale_one": scale_one,
        "hidden_one": hidden_one,
        "cos": cos_table,
        "sin": sin_table,
        "query_rot": query_rot,
        "key_rot": key_rot,
        "values": values,
        "allowed": allowed,
        "log_total": log_total,
        "attended": attended,
        "normed_two": normed_two,
        "scale_two": scale_two,
        "hidden_two": hidden_two,
        "gate": gate,
        "up_proj": up_proj,
        "activ": activ,
    }
    return (saved, result)


def backward_ffn(saved, cotangent, weights):
    w_gate, w_up, w_down, gain_ffn = (weights[4], weights[5], weights[6], weights[8])
    gate, up_proj = (saved["gate"], saved["up_proj"])
    d_act = jnp.dot(cotangent, w_down.T, preferred_element_type=jnp.float32)
    sigmoid_gate = jax.nn.sigmoid(gate)
    d_gate = (d_act * up_proj * sigmoid_gate * (1.0 + gate * (1.0 - sigmoid_gate))).astype(
        jnp.bfloat16
    )
    d_up = (d_act * gate * sigmoid_gate).astype(jnp.bfloat16)
    d_hidden = jnp.dot(d_gate, w_gate.T, preferred_element_type=jnp.float32)
    d_hidden = d_hidden + jnp.dot(d_up, w_up.T, preferred_element_type=jnp.float32)
    d_normed, gain_two_part = rms_backward(
        d_hidden, saved["normed_two"], saved["scale_two"], gain_ffn
    )
    d_mixed = cotangent.astype(jnp.float32) + d_normed
    return (d_mixed, d_gate, d_up, gain_two_part)


def backward_attn(saved, d_mixed, weights):
    w_query, w_key, w_value, w_output, gain_attn = (
        weights[0],
        weights[1],
        weights[2],
        weights[3],
        weights[7],
    )
    query_rot, key_rot, values = (saved["query_rot"], saved["key_rot"], saved["values"])
    batch, count, kv_heads, group, head_dim = query_rot.shape
    rows = batch * count
    d_attn = d_mixed.astype(jnp.bfloat16)
    d_out = jnp.dot(d_attn, w_output.T, preferred_element_type=jnp.float32).astype(jnp.bfloat16)
    d_out = d_out.reshape(batch, count, kv_heads, group, head_dim)
    probs = attention_probs(query_rot, key_rot, saved["allowed"], saved["log_total"])
    probs_low = probs.astype(jnp.bfloat16)
    d_vals = mult("bkgqt,bqkgd->btkd", probs_low, d_out)
    d_probs = mult("bqkgd,btkd->bkgqt", d_out, values)
    row_dot = jnp.sum(probs * d_probs, axis=-1, keepdims=True)
    d_scores = (probs * (d_probs - row_dot) * 0.125).astype(jnp.bfloat16)
    d_query = mult("bkgqt,btkd->bqkgd", d_scores, key_rot).reshape(
        batch, count, kv_heads * group, head_dim
    )
    d_keys = mult("bkgqt,bqkgd->btkd", d_scores, query_rot)
    d_query = unrotate(d_query, saved["cos"], saved["sin"]).astype(jnp.bfloat16).reshape(rows, -1)
    d_keys = unrotate(d_keys, saved["cos"], saved["sin"]).astype(jnp.bfloat16).reshape(rows, -1)
    d_vals = d_vals.astype(jnp.bfloat16).reshape(rows, -1)
    d_hidden = jnp.dot(d_query, w_query.T, preferred_element_type=jnp.float32)
    d_hidden = d_hidden + jnp.dot(d_keys, w_key.T, preferred_element_type=jnp.float32)
    d_hidden = d_hidden + jnp.dot(d_vals, w_value.T, preferred_element_type=jnp.float32)
    d_normed, gain_one_part = rms_backward(
        d_hidden, saved["normed_one"], saved["scale_one"], gain_attn
    )
    grad_in = (d_mixed + d_normed).astype(jnp.bfloat16)
    return (grad_in, d_attn, d_query, d_keys, d_vals, gain_one_part)


def local(
    inputs,
    seg_ids,
    cotangent,
    w_query,
    w_key,
    w_value,
    w_output,
    w_gate,
    w_up,
    w_down,
    gain_attn,
    gain_ffn,
):
    weights = (
        lax.all_gather(w_query, "shard", axis=0, tiled=True),
        lax.all_gather(w_key, "shard", axis=0, tiled=True),
        lax.all_gather(w_value, "shard", axis=0, tiled=True),
        lax.all_gather(w_output, "shard", axis=0, tiled=True),
        lax.all_gather(w_gate, "shard", axis=0, tiled=True),
        lax.all_gather(w_up, "shard", axis=0, tiled=True),
        lax.all_gather(w_down, "shard", axis=0, tiled=True),
        lax.all_gather(gain_attn.astype(jnp.bfloat16), "shard", axis=0, tiled=True).astype(
            gain_attn.dtype
        ),
        lax.all_gather(gain_ffn.astype(jnp.bfloat16), "shard", axis=0, tiled=True).astype(
            gain_ffn.dtype
        ),
    )
    segments = seg_ids[None, :]
    saved, result = forward(inputs, segments, weights, H, KVH)
    weights_back = (
        lax.all_gather(w_query, "shard", axis=0, tiled=True),
        lax.all_gather(w_key, "shard", axis=0, tiled=True),
        lax.all_gather(w_value, "shard", axis=0, tiled=True),
        lax.all_gather(w_output, "shard", axis=0, tiled=True),
        lax.all_gather(w_gate, "shard", axis=0, tiled=True),
        lax.all_gather(w_up, "shard", axis=0, tiled=True),
        lax.all_gather(w_down, "shard", axis=0, tiled=True),
        lax.all_gather(gain_attn.astype(jnp.bfloat16), "shard", axis=0, tiled=True).astype(
            gain_attn.dtype
        ),
        lax.all_gather(gain_ffn.astype(jnp.bfloat16), "shard", axis=0, tiled=True).astype(
            gain_ffn.dtype
        ),
    )
    d_mixed, d_gate, d_up, gain_two_part = backward_ffn(saved, cotangent, weights_back)
    grad_in, d_attn, d_query, d_keys, d_vals, gain_one_part = backward_attn(
        saved, d_mixed, weights_back
    )
    hidden_one, hidden_two = (saved["hidden_one"], saved["hidden_two"])
    attended, activ = (saved["attended"], saved["activ"])
    query_part = jnp.dot(hidden_one.T, d_query, preferred_element_type=jnp.float32)
    key_part = jnp.dot(hidden_one.T, d_keys, preferred_element_type=jnp.float32)
    value_part = jnp.dot(hidden_one.T, d_vals, preferred_element_type=jnp.float32)
    output_part = jnp.dot(attended.T, d_attn, preferred_element_type=jnp.float32)
    gate_part = jnp.dot(hidden_two.T, d_gate, preferred_element_type=jnp.float32)
    up_part = jnp.dot(hidden_two.T, d_up, preferred_element_type=jnp.float32)
    down_part = jnp.dot(activ.T, cotangent, preferred_element_type=jnp.float32)
    summed_rows = (
        lax.psum_scatter(
            query_part.astype(jnp.bfloat16), "shard", scatter_dimension=0, tiled=True
        ).astype(jnp.float32),
        lax.psum_scatter(
            key_part.astype(jnp.bfloat16), "shard", scatter_dimension=0, tiled=True
        ).astype(jnp.float32),
        lax.psum_scatter(
            value_part.astype(jnp.bfloat16), "shard", scatter_dimension=0, tiled=True
        ).astype(jnp.float32),
        lax.psum_scatter(
            output_part.astype(jnp.bfloat16), "shard", scatter_dimension=0, tiled=True
        ).astype(jnp.float32),
        lax.psum_scatter(
            gate_part.astype(jnp.bfloat16), "shard", scatter_dimension=0, tiled=True
        ).astype(jnp.float32),
        lax.psum_scatter(
            up_part.astype(jnp.bfloat16), "shard", scatter_dimension=0, tiled=True
        ).astype(jnp.float32),
        lax.psum_scatter(
            down_part.astype(jnp.bfloat16), "shard", scatter_dimension=0, tiled=True
        ).astype(jnp.float32),
        lax.psum_scatter(
            gain_one_part.astype(jnp.bfloat16), "shard", scatter_dimension=0, tiled=True
        ).astype(jnp.float32),
        lax.psum_scatter(
            gain_two_part.astype(jnp.bfloat16), "shard", scatter_dimension=0, tiled=True
        ).astype(jnp.float32),
    )
    (
        row_query,
        row_key,
        row_value,
        row_output,
        row_gate,
        row_up,
        row_down,
        row_gain_one,
        row_gain_two,
    ) = summed_rows
    totals = (
        lax.psum(row_query.astype(jnp.bfloat16), "rep").astype(jnp.float32),
        lax.psum(row_key.astype(jnp.bfloat16), "rep").astype(jnp.float32),
        lax.psum(row_value.astype(jnp.bfloat16), "rep").astype(jnp.float32),
        lax.psum(row_output.astype(jnp.bfloat16), "rep").astype(jnp.float32),
        lax.psum(row_gate.astype(jnp.bfloat16), "rep").astype(jnp.float32),
        lax.psum(row_up.astype(jnp.bfloat16), "rep").astype(jnp.float32),
        lax.psum(row_down.astype(jnp.bfloat16), "rep").astype(jnp.float32),
        lax.psum(row_gain_one.astype(jnp.bfloat16), "rep").astype(jnp.float32),
        lax.psum(row_gain_two.astype(jnp.bfloat16), "rep").astype(jnp.float32),
    )
    (
        grad_query,
        grad_key,
        grad_value,
        grad_output,
        grad_gate,
        grad_up,
        grad_down,
        grad_gain_attn,
        grad_gain_ffn,
    ) = totals
    return (
        result,
        grad_in,
        grad_query,
        grad_key,
        grad_value,
        grad_output,
        grad_gate,
        grad_up,
        grad_down,
        grad_gain_attn,
        grad_gain_ffn,
    )


def solution(mesh):
    placed = (
        P(("rep", "shard"), None),
        P(("rep", "shard")),
        P(("rep", "shard"), None),
        P("shard", None),
        P("shard", None),
        P("shard", None),
        P("shard", None),
        P("shard", None),
        P("shard", None),
        P("shard", None),
        P("shard"),
        P("shard"),
    )
    return jax.shard_map(
        local,
        mesh=mesh,
        in_specs=placed,
        out_specs=(
            P(("rep", "shard"), None),
            P(("rep", "shard"), None),
            P("shard", None),
            P("shard", None),
            P("shard", None),
            P("shard", None),
            P("shard", None),
            P("shard", None),
            P("shard", None),
            P("shard"),
            P("shard"),
        ),
        check_vma=False,
    )
```

profile of v0, /device:TPU:35, one launch (start us, length us, event | category | flops | bytes accessed | tf_op | source)
XLA Modules:
  0.0 725.8 jit_solution(11560137670754930847)
XLA Ops:
  14.4 28.4 %all-reduce.17 = (bf16[960]{0:T(1024)(128)(2,1)S(1)}, bf16[960]{0:T(1024)(128)(2,1)S(1)}) all-reduce(bf16[960]{0:T(1024)(128)(2,1)S(1)} %dynamic-update-slice, bf16[960]{0:T(1024)(128)(2,1)S(1)} %dynamic-update-slice.1), channel_id=1, replica_groups=mesh['rep'=8,'shard'=16] {'shard'}, use_global_device_ids=true, to_apply=%add | all-reduce | flops 1920 | bytes 7680
  42.9 23.9 %all-gather.1 = bf16[16,60,320]{2,1,0:T(8,128)(2,1)S(1)} all-gather(bf16[1,60,320]{2,1,0:T(8,128)(2,1)} %bitcast.187), channel_id=1, replica_groups=mesh['rep'=8,'shard'=16] {'shard'}, dimensions={0}, use_global_device_ids=true | all-gather | bytes 652800 | tf_op jit(solution)/shard_map/all_gather | solution.py:207
  67.1 17.5 %all-gather = bf16[16,60,320]{2,1,0:T(8,128)(2,1)S(1)} all-gather(bf16[1,60,320]{2,1,0:T(8,128)(2,1)} %bitcast.188), channel_id=1, replica_groups=mesh['rep'=8,'shard'=16] {'shard'}, dimensions={0}, use_global_device_ids=true | all-gather | bytes 652800 | tf_op jit(solution)/shard_map/all_gather | solution.py:208
  88.3 3.9 reshape.396
  92.3 11.4 %all-gather.16.cloned.1.call-done = bf16[16,60,960]{2,1,0:T(8,128)(2,1)} async-done(((bf16[1,60,960]{2,1,0:T(8,128)(2,1)}), bf16[16,60,960]{2,1,0:T(8,128)(2,1)}) %all-gather.16.cloned.1.call-update) | async-done | bytes 1843216 | tf_op jit(solution)/shard_map/all_gather | solution.py:209
  116.2 46.4 %all-gather.18.cloned.1.call-done = bf16[16,60,2560]{2,1,0:T(8,128)(2,1)} async-done(((bf16[1,60,2560]{2,1,0:T(8,128)(2,1)}), bf16[16,60,2560]{2,1,0:T(8,128)(2,1)}) %all-gather.18.cloned.1.call-update) | async-done | bytes 4915216 | tf_op jit(solution)/shard_map/all_gather | solution.py:210
  162.5 7.4 %reshape.400 = bf16[960,2560]{1,0:T(8,128)(2,1)} reshape(bf16[16,60,2560]{2,1,0:T(8,128)(2,1)} %all-gather.18.cloned.1.call-done) | data formatting | bytes 9830400
  169.9 50.7 %all-gather.20.cloned.1.call-done = bf16[16,60,2560]{2,1,0:T(8,128)(2,1)} async-done(((bf16[1,60,2560]{2,1,0:T(8,128)(2,1)}), bf16[16,60,2560]{2,1,0:T(8,128)(2,1)}) %all-gather.20.cloned.1.call-update) | async-done | bytes 4915216 | tf_op jit(solution)/shard_map/all_gather | solution.py:211
  220.6 7.4 %reshape.402 = bf16[960,2560]{1,0:T(8,128)(2,1)} reshape(bf16[16,60,2560]{2,1,0:T(8,128)(2,1)} %all-gather.20.cloned.1.call-done) | data formatting | bytes 9830400
  228.0 5.6 fusion.59
  236.7 42.0 %all-gather.12.cloned.1.call-done = bf16[2560,960]{1,0:T(8,128)(2,1)} async-done(((bf16[160,960]{1,0:T(8,128)(2,1)}), bf16[2560,960]{1,0:T(8,128)(2,1)}) %all-gather.12.cloned.1.call-update) | async-done | bytes 4915216 | tf_op jit(solution)/shard_map/all_gather | solution.py:212
  278.7 8.8 %multiply_convert_fusion = (bf16[256,2560]{1,0:T(8,128)(2,1)}, bf16[256,2560]{1,0:T(8,128)(2,1)}, bf16[256,2560]{1,0:T(8,128)(2,1)S(1)}) fusion(f32[256,2560]{1,0:T(8,128)} %fusion.59, f32[256,2560]{1,0:T(8,128)} %fusion.60, bf16[256,960]{0,1:T(8,128)(2,1)S(1)} %copy-done.11, bf16[2560,960]{1,0:T(8,128)(2,1)} %all-gather.12.cloned.1.call-done), kind=kOutput, calls=%fused_computation.18 | convolution fusion | flops 1268776960 | bytes 14581760 | tf_op jit(solution)/shard_map/dot_general | solution.py:139
  288.5 3.9 convolution_convert_fusion
  294.0 4.4 fusion.61
  314.7 3.6 convolution_convert_fusion.1
  318.3 3.6 convolution_convert_fusion.2
  322.0 190.7 %fusion.57 = (bf16[64,960]{1,0:T(8,128)(2,1)}, bf16[64,960]{1,0:T(8,128)(2,1)S(1)}, bf16[64,2560]{1,0:T(8,128)(2,1)}, bf16[64,2560]{1,0:T(8,128)(2,1)}, bf16[64,...) fusion(bf16[960,960]{1,0:T(8,128)(2,1)} %convolution_convert_fusion.4, bf16[960,960]{1,0:T(8,128)(2,1)} %convolution_convert_fusion.3, ...), kind=kCustom, calls=%all-reduce-scatter.6 | all-reduce-scatter fusion | flops 7864321 | bytes 15729152
  523.8 5.4 collective-permute-start.3
  532.6 30.6 %all-reduce.16 = (bf16[960]{0:T(1024)(128)(2,1)}, bf16[960]{0:T(1024)(128)(2,1)}) all-reduce(bf16[960]{0:T(1024)(128)(2,1)S(1)} %get-tuple-element.13, bf16[960]{0:T(1024)(128)(2,1)} %get-tuple-element.11), channel_id=9, replica_groups=mesh['rep'=8,'shard'=16] {'shard'}, use_global_device_ids=true, to_apply=%region_23.24.clone | all-reduce | flops 1920 | bytes 7680
  590.7 5.8 concatenate.50
  598.3 5.8 concatenate.49
  606.9 5.8 fusion.23
  612.7 32.1 %all-reduce.24.cloned.1.call-done = (bf16[60,320]{1,0:T(8,128)(2,1)}, bf16[60,320]{1,0:T(8,128)(2,1)}, bf16[60]{0:T(256)(128)(2,1)}, bf16[60]{0:T(256)(128)(2,1)}) async-done(((bf16[60,320]{1,0:T(8,128)(2,1)}, bf16[60,320]{1,0:T(8,128)(2,1)}, bf16[60]{0:T(256)(128)(2,1)}, bf16[60]{0:T(256)(128)(2,1)}), (bf16[60,320]{1,0:T(8,128)(2,1)}, bf16[60,320]{1,0:T(8,128)(2,1)}, bf16[60]{0:T(256)(128)(2,1)}, ...) | async-done | bytes 77056 | tf_op jit(solution)/shard_map/psum | solution.py:292
  650.0 60.2 %all-reduce.26.cloned.1.call-done = (bf16[60,960]{1,0:T(8,128)(2,1)}, bf16[60,960]{1,0:T(8,128)(2,1)}, bf16[60,2560]{1,0:T(8,128)(2,1)}, bf16[60,2560]{1,0:T(8,128)(2,1)}, bf16[160,960]{1,0:T(8,128)(2,1)}) async-done(((bf16[60,960]{1,0:T(8,128)(2,1)}, bf16[60,960]{1,0:T(8,128)(2,1)}, bf16[60,2560]{1,0:T(8,128)(2,1)}, bf16[60,2560]{1,0:T(8,128)(2,1)}, bf16[160,960]{1,0:T(8,128)(2,1)}), ...) | async-done | bytes 1152016 | tf_op jit(solution)/shard_map/psum | solution.py:291
  (185 shorter events, 103.8 us)
Async XLA Ops:
  7.2 77.8 %copy-start.34 = (s32[256]{0:T(256)S(1)}, s32[256]{0:T(256)}, u32[]{:S(2)}) copy-start(s32[256]{0:T(256)} %param.13) | copy-start | bytes 3076
  7.2 78.0 %copy-start.3 = (bf16[256,960]{0,1:T(8,128)(2,1)S(1)}, bf16[256,960]{0,1:T(8,128)(2,1)}, u32[]{:S(2)}) copy-start(bf16[256,960]{0,1:T(8,128)(2,1)} %param.12) | copy-start | bytes 1474564
  7.2 81.1 %all-gather.14.cloned.1.call-start = ((), (), s32[]{:S(2)}) async-start(), calls=%async_computation.3 | async-start | bytes 2228224 | tf_op jit(solution)/shard_map/all_gather | solution.py:206
  7.9 95.7 %all-gather.16.cloned.1.call-start = ((), (), s32[]{:S(2)}) async-start(), calls=%async_computation.4 | async-start | bytes 2228224 | tf_op jit(solution)/shard_map/all_gather | solution.py:209
  8.7 153.9 %all-gather.18.cloned.1.call-start = ((), (), s32[]{:S(2)}) async-start(), calls=%async_computation.5 | async-start | bytes 5570560 | tf_op jit(solution)/shard_map/all_gather | solution.py:210
  9.4 211.2 %all-gather.20.cloned.1.call-start = ((), (), s32[]{:S(2)}) async-start(), calls=%async_computation.6 | async-start | bytes 5570560 | tf_op jit(solution)/shard_map/all_gather | solution.py:211
  10.0 268.7 %all-gather.12.cloned.1.call-start = ((), (), s32[]{:S(2)}) async-start(), calls=%async_computation.1 | async-start | bytes 5570560 | tf_op jit(solution)/shard_map/all_gather | solution.py:212
  10.6 595.2 %reduce-scatter.14.cloned.1.call-start = ((), (), s32[]{:S(2)}) async-start(), calls=%async_computation.2 | async-start | bytes 5570560 | tf_op jit(solution)/shard_map/reduce_scatter | solution.py:269
  67.1 25.1 %copy-start.9 = (bf16[960,320]{1,0:T(8,128)(2,1)}, bf16[960,320]{1,0:T(8,128)(2,1)S(1)}, u32[]{:S(2)}) copy-start(bf16[960,320]{1,0:T(8,128)(2,1)S(1)} %reshape.394) | copy-start | bytes 1843204
  106.4 8.6 %copy-start.4 = (bf16[960,960]{1,0:T(8,128)(2,1)}, bf16[960,960]{1,0:T(8,128)(2,1)S(1)}, u32[]{:S(2)}) copy-start(bf16[960,960]{1,0:T(8,128)(2,1)S(1)} %reshape.398) | copy-start | bytes 5529604
  233.6 45.1 %copy-start.11 = (bf16[256,960]{0,1:T(8,128)(2,1)S(1)}, bf16[256,960]{0,1:T(8,128)(2,1)}, u32[]{:S(2)}) copy-start(bf16[256,960]{0,1:T(8,128)(2,1)} %param.14) | copy-start | bytes 1474564
  292.4 352.4 %all-reduce.24.cloned.1.call-start = ((), (), s32[]{:S(2)}) async-start(), calls=%async_computation.7 | async-start | bytes 198656 | tf_op jit(solution)/shard_map/psum | solution.py:292
  512.7 18.8 %copy-start.15 = (bf16[64,960]{1,0:T(8,128)(2,1)}, bf16[64,960]{1,0:T(8,128)(2,1)S(1)}, u32[]{:S(2)}) copy-start(bf16[64,960]{1,0:T(8,128)(2,1)S(1)} %get-tuple-element.35) | copy-start | bytes 368644
  512.7 18.8 %copy-start.10 = (bf16[960,320]{1,0:T(8,128)(2,1)S(1)}, bf16[960,320]{1,0:T(8,128)(2,1)}, u32[]{:S(2)}) copy-start(bf16[960,320]{1,0:T(8,128)(2,1)} %copy-done.9) | copy-start | bytes 1843204
  512.7 18.8 %copy-start.23 = (bf16[1,256,5,64]{1,3,2,0:T(8,128)(2,1)S(1)}, bf16[1,256,5,64]{1,3,2,0:T(8,128)(2,1)}, u32[]{:S(2)}) copy-start(bf16[1,256,5,64]{1,3,2,0:T(8,128)(2,1)} %copy-done.22) | copy-start | bytes 491524
  513.4 57.2 %collective-permute-start.2 = (bf16[60,320]{1,0:T(8,128)(2,1)}, bf16[60,320]{1,0:T(8,128)(2,1)}, u32[]{:S(2)}, u32[]{:S(2)}) collective-permute-start(bf16[60,320]{1,0:T(8,128)(2,1)} %slice.42), channel_id=1, source_target_pairs={{0,1},{1,2},{2,3},{3,4},{4,5},{5,6},{6,7},{7,8},{8,9},{9,10},{10,1... | collective-permute-start | bytes 115208
  517.1 73.6 %collective-permute-start.5 = (bf16[60,2560]{1,0:T(8,128)(2,1)}, bf16[60,2560]{1,0:T(8,128)(2,1)}, u32[]{:S(2)}, u32[]{:S(2)}) collective-permute-start(bf16[60,2560]{1,0:T(8,128)(2,1)} %slice.45), channel_id=1, source_target_pairs={{0,1},{1,2},{2,3},{3,4},{4,5},{5,6},{6,7},{7,8},{8,9},{9,10},{10,1... | collective-permute-start | bytes 921608
  520.8 77.4 %collective-permute-start.4 = (bf16[60,2560]{1,0:T(8,128)(2,1)}, bf16[60,2560]{1,0:T(8,128)(2,1)}, u32[]{:S(2)}, u32[]{:S(2)}) collective-permute-start(bf16[60,2560]{1,0:T(8,128)(2,1)} %slice.44), channel_id=1, source_target_pairs={{0,1},{1,2},{2,3},{3,4},{4,5},{5,6},{6,7},{7,8},{8,9},{9,10},{10,1... | collective-permute-start | bytes 921608
  523.8 8.2 %copy-start.8 = (bf16[960,320]{1,0:T(8,128)(2,1)S(1)}, bf16[960,320]{1,0:T(8,128)(2,1)}, u32[]{:S(2)}) copy-start(bf16[960,320]{1,0:T(8,128)(2,1)} %copy-done.7) | copy-start | bytes 1843204
  523.8 8.2 %copy-start.31 = (bf16[5,64,256]{2,1,0:T(8,128)(2,1)S(1)}, bf16[5,64,256]{2,1,0:T(8,128)(2,1)}, u32[]{:S(2)}) copy-start(bf16[5,64,256]{2,1,0:T(8,128)(2,1)} %copy-done.30) | copy-start | bytes 491524
  523.8 57.3 %collective-permute-start.3 = (bf16[60,960]{1,0:T(8,128)(2,1)}, bf16[60,960]{1,0:T(8,128)(2,1)}, u32[]{:S(2)}, u32[]{:S(2)}) collective-permute-start(bf16[60,960]{1,0:T(8,128)(2,1)} %slice.43), channel_id=1, source_target_pairs={{0,1},{1,2},{2,3},{3,4},{4,5},{5,6},{6,7},{7,8},{8,9},{9,10},{10,1... | collective-permute-start | bytes 345608
  566.3 10.4 %collective-permute-start.1 = (bf16[60,320]{1,0:T(8,128)(2,1)}, bf16[60,320]{1,0:T(8,128)(2,1)}, u32[]{:S(2)}, u32[]{:S(2)}) collective-permute-start(bf16[60,320]{1,0:T(8,128)(2,1)} %slice.41), channel_id=1, source_target_pairs={{0,1},{1,2},{2,3},{3,4},{4,5},{5,6},{6,7},{7,8},{8,9},{9,10},{10,1... | collective-permute-start | bytes 115208
  570.5 13.8 %collective-permute-start = (bf16[60,960]{1,0:T(8,128)(2,1)}, bf16[60,960]{1,0:T(8,128)(2,1)}, u32[]{:S(2)}, u32[]{:S(2)}) collective-permute-start(bf16[60,960]{1,0:T(8,128)(2,1)} %slice.40), channel_id=1, source_target_pairs={{0,1},{1,2},{2,3},{3,4},{4,5},{5,6},{6,7},{7,8},{8,9},{9,10},{10,1... | collective-permute-start | bytes 345608
  581.0 129.2 %all-reduce.26.cloned.1.call-start = ((), (), s32[]{:S(2)}) async-start(), calls=%async_computation.8 | async-start | bytes 2490368 | tf_op jit(solution)/shard_map/psum | solution.py:291
  (27 other events, 85.2 us)
Sparse Core Ops, SparseCore 0:
  10.2 45.9 all-gather.13
  58.3 45.3 all-gather.15
  105.8 56.7 all-gather.17
  164.5 56.0 all-gather.19
  222.6 56.0 all-gather.11
  292.5 241.5 reduce-scatter.13
  581.1 63.6 all-reduce.23
  648.3 61.8 all-reduce.25
where the time goes:
time: 733 us; the launch traced here: 726 us
  blocking collectives  291 us (40%)
  waiting for transfers between devices  246 us (34%)
  local copies, waits for them, and re-layouts  70.2 us (10%)
  matrix products  63.7 us (9%)
  other arithmetic  21.4 us (3%)
  between operations  16.7 us (2%)
  starting transfers between devices  16.5 us (2%)
    unnamed x3, blocking collectives  250 us
    unnamed x105, local copies, waits for them, and re-layouts  70.2 us
    psum x1, waiting for transfers between devices, local(): lax.psum(row_query.astype(jnp.bfloat16), 'rep').astype(jnp.float32)  60.2 us
    all_gather x1, waiting for transfers between devices, local(): lax.all_gather(w_up, 'shard', axis=0, tiled=True)  50.7 us
    all_gather x1, waiting for transfers between devices, local(): lax.all_gather(w_gate, 'shard', axis=0, tiled=True)  46.4 us
    all_gather x1, waiting for transfers between devices, local(): lax.all_gather(w_down, 'shard', axis=0, tiled=True)  42 us
    psum x1, waiting for transfers between devices, local(): lax.psum(row_key.astype(jnp.bfloat16), 'rep').astype(jnp.float32)  32.1 us
    all_gather x1, blocking collectives, local(): lax.all_gather(w_key, 'shard', axis=0, tiled=True)  23.9 us
  transfers between devices with their start and end apart: 14, of which 6 were waited for; matrix products, arithmetic and copies ran while one was open for 44% of the time, Pallas kernels for 0%

commit v1 on v0

v1 whole, which is shorter than its diff:
```python
import jax
import jax.numpy as jnp
from jax import lax
from jax.sharding import PartitionSpec as P

H = 15
KVH = 5
HD = 64
D = 960
QK = 1280
FF = 2560
EPSILON = 1e-05
THETA = 100000.0
F32 = jnp.float32
BF = jnp.bfloat16
AX = ("rep", "shard")


def device(x, c, z, y):
    return ((x % 4) * 2 + c % 2) * 16 + (z % 4) * 4 + y % 4


def shift(value, axis, step):
    move = {"x": 0, "c": 0, "z": 0, "y": 0, axis: step}
    pairs = [
        (device(x, c, z, y), device(x + move["x"], c + move["c"], z + move["z"], y + move["y"]))
        for x in range(4)
        for c in range(2)
        for z in range(4)
        for y in range(4)
    ]
    return lax.ppermute(value, AX, pairs)


def dot(left, right):
    return jnp.dot(left, right, preferred_element_type=F32)


def dot_t(left, right):
    return lax.dot_general(left, right, (((1,), (1,)), ((), ())), preferred_element_type=F32)


def t_dot(left, right):
    return lax.dot_general(left, right, (((0,), (0,)), ((), ())), preferred_element_type=F32)


def collect(value, axis):
    return [value] + [shift(value, axis, -step) for step in (1, 2, 3)]


def spread(blocks, axis):
    got = [shift(blocks[step], axis, step) for step in (1, 2, 3)]
    total = blocks[0].astype(F32)
    for part in got:
        total = total + part.astype(F32)
    return total.astype(BF)


def gather_rel(value, first, second):
    inner = jnp.concatenate(collect(value, first), axis=0)
    mine = jnp.concatenate(collect(inner, second), axis=0)
    return jnp.concatenate([mine, shift(mine, "c", 1)], axis=0)


def gather_abs(value, first, second, where):
    rows, cols = value.shape
    inner = jnp.zeros((4, rows, cols), BF)
    for step, part in enumerate(collect(value, first)):
        inner = lax.dynamic_update_slice(inner, part[None], ((where[first] + step) % 4, 0, 0))
    mine = jnp.zeros((4, 4, rows, cols), BF)
    for step, part in enumerate(collect(inner, second)):
        at = (where[second] + step) % 4
        if second == "z":
            mine = lax.dynamic_update_slice(mine, part[None], (at, 0, 0, 0))
        else:
            mine = lax.dynamic_update_slice(mine, part[:, None], (0, at, 0, 0))
    other = shift(mine, "c", 1)
    low = where["c"] == 0
    both = jnp.stack([jnp.where(low, mine, other), jnp.where(low, other, mine)], axis=2)
    return both.reshape(32 * rows, cols)


def scatter_rel(own, other, first, second):
    total = (own + shift(other.astype(BF), "c", 1).astype(F32)).astype(BF)
    cols = total.shape[1]
    total = total.reshape(4, -1, cols)
    total = spread([total[i] for i in range(4)], first)
    total = total.reshape(4, -1, cols)
    return spread([total[i] for i in range(4)], second)


def scatter_abs(value, first, second, where):
    rows = value.shape[0] // 32
    cols = value.shape[1]
    value = value.reshape(4, 4, 2, rows, cols)
    own = lax.dynamic_index_in_dim(value, where["c"], 2, keepdims=False)
    other = lax.dynamic_index_in_dim(value, 1 - where["c"], 2, keepdims=False)
    total = (own.astype(F32) + shift(other, "c", 1).astype(F32)).astype(BF)
    dim = 0 if first == "z" else 1
    total = spread(
        [
            lax.dynamic_index_in_dim(total, (where[first] + i) % 4, dim, keepdims=False)
            for i in range(4)
        ],
        first,
    )
    return spread(
        [
            lax.dynamic_index_in_dim(total, (where[second] + i) % 4, 0, keepdims=False)
            for i in range(4)
        ],
        second,
    )


def finish(part, where):
    one, two, three = [shift(part, "x", step) for step in (1, 2, 3)]
    total = (part.astype(F32) + two.astype(F32)) + (one.astype(F32) + three.astype(F32))
    total = total.astype(BF)
    other = shift(total, "c", 1)
    low = where["c"] == 0
    return jnp.concatenate(
        [jnp.where(low, total, other), jnp.where(low, other, total)], axis=0
    ).astype(F32)


def order_matrix(where, major, minor):
    place = lax.broadcasted_iota(jnp.int32, (D, 1024), 1)
    natural = lax.broadcasted_iota(jnp.int32, (D, 1024), 0)
    core = (where["c"] + place // 512) % 2
    at = {
        major: (where[major] + (place // 128) % 4) % 4,
        minor: (where[minor] + (place // 32) % 4) % 4,
    }
    inner = core * 32 + place % 32
    target = (at["z"] * 4 + at["y"]) * 60 + inner
    return ((target == natural) & (inner < 60)).astype(BF)


def rotary_tables(segments):
    count = segments.shape[0]
    index = jnp.arange(count, dtype=jnp.int32)
    same = segments[:, None] == segments[None, :]
    first = jnp.min(jnp.where(same, index[None, :], count), axis=-1)
    position = (index - first).astype(F32)
    half = HD // 2
    freq = THETA ** (-jnp.arange(half, dtype=F32) / half)
    angle = position[:, None] * freq
    return (jnp.cos(angle)[:, None, :], jnp.sin(angle)[:, None, :])


def rotate(values, cos, sin):
    a, b = (values[..., : HD // 2], values[..., HD // 2 :])
    return jnp.concatenate([a * cos - b * sin, b * cos + a * sin], axis=-1)


def unrotate(values, cos, sin):
    a, b = (values[..., : HD // 2], values[..., HD // 2 :])
    return jnp.concatenate([a * cos + b * sin, b * cos - a * sin], axis=-1)


def mult(form, left, right):
    return jnp.einsum(form, left, right, preferred_element_type=F32)


def norm(values):
    scale = lax.rsqrt(jnp.mean(values * values, axis=-1, keepdims=True) + EPSILON)
    return (values * scale, scale)


def norm_back(e, normed, scale):
    return scale * (e - normed * jnp.mean(e * normed, axis=-1, keepdims=True))


def half_rows(value, where):
    padded = jnp.pad(value, ((0, 4), (0, 0)))
    return lax.dynamic_slice_in_dim(padded, where["c"] * 32, 32, 0)


def local(x, seg, dy, wq, wk, wv, wo, wg, wu, wd, gain_a, gain_f):
    rep = lax.axis_index("rep")
    shard = lax.axis_index("shard")
    where = {"c": rep % 2, "z": shard // 4, "y": shard % 4}
    ga = gain_a[:, None]
    gf = gain_f[:, None]
    scaled = lambda w, g: (w.astype(F32) * g).astype(BF)
    s_qk = half_rows(jnp.concatenate([scaled(wq, ga), scaled(wk, ga)], axis=1), where)
    s_ov = half_rows(jnp.concatenate([wo, scaled(wv, ga)], axis=1), where)
    s_g = half_rows(scaled(wg, gf), where)
    s_u = half_rows(scaled(wu, gf), where)
    s_d = lax.dynamic_slice_in_dim(wd, where["c"] * 80, 80, 0)
    w_qk = gather_rel(s_qk, "y", "z")
    w_ov = gather_rel(s_ov, "z", "y")
    w_g = gather_rel(s_g, "y", "z")
    w_u = gather_rel(s_u, "z", "y")
    w_d1 = gather_abs(s_d[:, :512], "y", "z", where)
    w_d2 = gather_abs(s_d[:, 512:], "z", "y", where)
    e1 = order_matrix(where, "z", "y")
    e2 = order_matrix(where, "y", "z")

    xf = x.astype(F32)
    n1, r1 = norm(xf)
    h1 = n1.astype(BF)
    h1a = dot(h1, e1).astype(BF)
    h1b = dot(h1, e2).astype(BF)
    cos, sin = rotary_tables(seg)
    qk = dot(h1a, w_qk)
    values = dot(h1b, w_ov)[:, D:].astype(BF).reshape(256, KVH, HD)
    qr = rotate(qk[:, :D].reshape(256, H, HD), cos, sin).astype(BF).reshape(256, KVH, 3, HD)
    kr = rotate(qk[:, D:].reshape(256, KVH, HD), cos, sin).astype(BF)
    index = jnp.arange(256, dtype=jnp.int32)
    allowed = (seg[:, None] == seg[None, :]) & (index[:, None] >= index[None, :])
    allowed = allowed[None, None]
    scores = mult("qkgd,tkd->kgqt", qr, kr) * 0.125
    row_max = jnp.max(jnp.where(allowed, scores, -1e30), axis=-1, keepdims=True)
    weight = jnp.where(allowed, jnp.exp(scores - row_max), 0.0)
    probs = weight / jnp.sum(weight, axis=-1, keepdims=True)
    pb = probs.astype(BF)
    att = mult("kgqt,tkd->qkgd", pb, values).astype(BF).reshape(256, D)
    att_b = dot(att, e2).astype(BF)
    w_o = w_ov[:, :D]
    mixed = xf + dot(att_b, w_o)

    n2, r2 = norm(mixed)
    h2 = n2.astype(BF)
    h2a = dot(h2, e1).astype(BF)
    h2b = dot(h2, e2).astype(BF)
    gate = dot(h2a, w_g)
    up = dot(h2b, w_u)
    sig = jax.nn.sigmoid(gate)
    act = (gate * sig * up).astype(BF)
    out = jnp.concatenate(
        [mixed[:, :512] + dot(act, w_d1), mixed[:, 512:] + dot(act, w_d2)], axis=1
    ).astype(BF)

    g_d1 = t_dot(act, dy[:, :512]).astype(BF)
    g_d2 = t_dot(act, dy[:, 512:]).astype(BF)
    t_d1 = finish(scatter_abs(g_d1, "z", "y", where), where)
    t_d2 = finish(scatter_abs(g_d2, "y", "z", where), where)
    d_act = dot_t(dy[:, :512], w_d1) + dot_t(dy[:, 512:], w_d2)
    d_gate = (d_act * up * sig * (1.0 + gate * (1.0 - sig))).astype(BF)
    d_up = (d_act * gate * sig).astype(BF)
    t_g = finish(
        scatter_rel(t_dot(h2a[:, :512], d_gate), t_dot(h2a[:, 512:], d_gate), "z", "y"), where
    )
    t_u = finish(
        scatter_rel(t_dot(h2b[:, :512], d_up), t_dot(h2b[:, 512:], d_up), "y", "z"), where
    )
    e_f = dot_t(dot_t(d_gate, w_g).astype(BF), e1) + dot_t(dot_t(d_up, w_u).astype(BF), e2)
    d_mixed = dy.astype(F32) + norm_back(e_f, n2, r2)

    d_attn = d_mixed.astype(BF)
    d_ob = dot_t(dot_t(d_attn, w_o).astype(BF), e2).astype(BF).reshape(256, KVH, 3, HD)
    d_vals = mult("kgqt,qkgd->tkd", pb, d_ob)
    d_p = mult("qkgd,tkd->kgqt", d_ob, values)
    row_dot = jnp.sum(probs * d_p, axis=-1, keepdims=True)
    d_s = (probs * (d_p - row_dot) * 0.125).astype(BF)
    d_q = mult("kgqt,tkd->qkgd", d_s, kr).reshape(256, H, HD)
    d_k = mult("kgqt,qkgd->tkd", d_s, qr)
    d_qk = jnp.concatenate(
        [
            unrotate(d_q, cos, sin).astype(BF).reshape(256, D),
            unrotate(d_k, cos, sin).astype(BF).reshape(256, 320),
        ],
        axis=1,
    )
    d_v = d_vals.astype(BF).reshape(256, 320)
    t_qk = finish(
        scatter_rel(t_dot(h1a[:, :512], d_qk), t_dot(h1a[:, 512:], d_qk), "z", "y"), where
    )
    g_ov = [
        jnp.concatenate([t_dot(att_b[:, s], d_attn), t_dot(h1b[:, s], d_v)], axis=1)
        for s in (slice(0, 512), slice(512, 1024))
    ]
    t_ov = finish(scatter_rel(g_ov[0], g_ov[1], "y", "z"), where)
    d_v_wide = jnp.pad(d_v, ((0, 0), (D, 0)))
    e_a = dot_t(dot_t(d_qk, w_qk).astype(BF), e1) + dot_t(dot_t(d_v_wide, w_ov).astype(BF), e2)
    grad_in = (d_mixed + norm_back(e_a, n1, r1)).astype(BF)

    t_qk, t_ov, t_g, t_u = (t_qk[:60], t_ov[:60], t_g[:60], t_u[:60])
    t_q, t_k, t_o, t_v = (t_qk[:, :D], t_qk[:, D:], t_ov[:, :D], t_ov[:, D:])
    rowsum = lambda w, t: jnp.sum(w.astype(F32) * t, axis=1)
    grad_ga = rowsum(wq, t_q) + rowsum(wk, t_k) + rowsum(wv, t_v)
    grad_gf = rowsum(wg, t_g) + rowsum(wu, t_u)
    t_d = jnp.concatenate([t_d1, t_d2], axis=1)
    return (
        out,
        grad_in,
        t_q * ga,
        t_k * ga,
        t_v * ga,
        t_o,
        t_g * gf,
        t_u * gf,
        t_d,
        grad_ga,
        grad_gf,
    )


def solution(mesh):
    token = P(("rep", "shard"), None)
    row = P("shard", None)
    return jax.shard_map(
        local,
        mesh=mesh,
        in_specs=(token, P(("rep", "shard")), token) + (row,) * 7 + (P("shard"),) * 2,
        out_specs=(token, token) + (row,) * 7 + (P("shard"),) * 2,
        check_vma=False,
    )
```

time: 733 us -> 550 us (0.75)
  blocking collectives: 291 us -> 0 us
  starting transfers between devices: 16.5 us -> 202 us
  waiting for transfers between devices: 246 us -> 120 us
  matrix products: 63.7 us -> 103 us
  other arithmetic: 21.4 us -> 38.6 us
  between operations: 16.7 us -> 3.29 us
    unnamed x3 -> x0, blocking collectives: 250 us -> none
    ppermute x0 -> x108, starting transfers between devices: none -> 202 us  [shift(): return lax.ppermute(value, AX, pairs)]
    all_gather x5 -> x0, waiting for transfers between devices: 150 us -> none  [the longest x1 50.7 us: local(): lax.all_gather(w_up, 'shard', axis=0, tiled=True)]
    ppermute x0 -> x108, waiting for transfers between devices: none -> 120 us  [shift(): return lax.ppermute(value, AX, pairs)]
    psum x2 -> x0, waiting for transfers between devices: 92.3 us -> none  [the longest x1 60.2 us: local(): lax.psum(row_query.astype(jnp.bfloat16), 'rep').astype(jnp.float32)]
    all_gather x2 -> x0, blocking collectives: 41.5 us -> none  [the longest x1 23.9 us: local(): lax.all_gather(w_key, 'shard', axis=0, tiled=True)]
    unnamed x105 -> x231, local copies, waits for them, and re-layouts: 70.2 us -> 32.8 us
    dot_general x27 -> x36, matrix products: 63.7 us -> 99.8 us  [the longest x7 31.2 us: dot_t(): lax.dot_general(left, right, (((1,), (1,)), ((), ())), preferred_element_...]
  transfers between devices with their start and end apart: 14 -> 108, of which waited for: 6 -> 34; matrix products, arithmetic and copies ran while one was open for 44% -> 24% of each run, Pallas kernels for 0% -> 0%
where the time goes in v1:
time: 550 us; the launch traced here: 539 us
  starting transfers between devices  202 us (37%)
  waiting for transfers between devices  120 us (22%)
  matrix products  103 us (19%)
  local copies, waits for them, and re-layouts  72.3 us (13%)
  other arithmetic  38.6 us (7%)
    ppermute x108, starting transfers between devices, shift(): return lax.ppermute(value, AX, pairs)  202 us
    ppermute x108, waiting for transfers between devices, shift(): return lax.ppermute(value, AX, pairs)  120 us
    unnamed x231, local copies, waits for them, and re-layouts  32.8 us
    dot_general x7, matrix products, dot_t(): lax.dot_general(left, right, (((1,), (1,)), ((), ())), preferred_element_...  31.2 us
    dot_general x12, matrix products, t_dot(): lax.dot_general(left, right, (((0,), (0,)), ((), ())), preferred_element_...  24.3 us
    dot_general x5, matrix products, mult(): return jnp.einsum(form, left, right, preferred_element_type=F32)  23.4 us
    dot_general x12, matrix products, dot(): return jnp.dot(left, right, preferred_element_type=F32)  20.8 us
    concatenate x4, local copies, waits for them, and re-layouts, gather_rel(): return jnp.concatenate([mine, shift(mine, 'c', 1)], axis=0)  12.5 us
  transfers between devices with their start and end apart: 108, of which 34 were waited for; matrix products, arithmetic and copies ran while one was open for 24% of the time, Pallas kernels for 0%

profile of v1, /device:TPU:35, one launch (start us, length us, event | category | flops | bytes accessed | tf_op | source)
XLA Modules:
  0.0 539.3 jit_solution(17804040412831888583)
XLA Ops:
  81.0 5.0 collective-permute-start.31
  91.5 12.0 %collective-permute-start.12 = (bf16[128,1280]{0,1:T(8,128)(2,1)S(1)}, bf16[128,1280]{0,1:T(8,128)(2,1)}, u32[]{:S(2)}, u32[]{:S(2)}) collective-permute-start(bf16[128,1280]{0,1:T(8,128)(2,1)S(1)} %pad_maximum_fusion.12), channel_id=1, source_target_pairs={{0,4},{1,5},{2,6},{3,7},{4,8},{5,9},{6,10},{7,11},{8,12},{9,13},{1... | collective-permute-start | bytes 983048 | tf_op jit(solution)/shard_map/ppermute | solution.py:32
  127.9 15.9 %collective-permute-start.41 = (bf16[4,4,80,448]{3,2,1,0:T(8,128)(2,1)S(1)}, bf16[4,4,80,448]{3,2,1,0:T(8,128)(2,1)S(1)}, u32[]{:S(2)}, u32[]{:S(2)}) collective-permute-start(bf16[4,4,80,448]{3,2,1,0:T(8,128)(2,1)S(1)} %bitcast_dynamic-update-slice_fusion.3), channel_id=1, source_target_pairs={{0,16},{1,17},{2,18},{3,19},{4,20},{5,21},{6,22},{7,23},{8,24},{9,... | collective-permute-start | bytes 3440648 | tf_op jit(solution)/shard_map/ppermute | solution.py:32
  161.5 5.9 %concatenate.116 = bf16[1024,1280]{0,1:T(8,128)(2,1)S(1)} concatenate(bf16[32,1280]{0,1:T(8,128)(2,1)S(1)} %fusion.88, bf16[32,1280]{0,1:T(8,128)(2,1)S(1)} %collective-permute-done.7, bf16[32,1280]{0,1:T(8,128)(2,1)} %copy-done.16, bf16[32,1280]{0,1:T(8,128)(2,1)} %copy-done.17, bf16[128,1280]{0,1:T(8,128)(2,1)} %copy-done.26, bf16[128,1280]{0,1:T(8,128)(2,1)} %copy-done.27, ...), dimensions={0} | concatenate | bytes 5242880 | tf_op jit(solution)/shard_map/concatenate | solution.py:62
  208.0 7.1 %fusion.65 = f32[256,960]{0,1:T(8,128)} fusion(bf16[256,2560]{1,0:T(8,128)(2,1)} %get-tuple-element.37, bf16[1024,2560]{1,0:T(8,128)(2,1)} %copy-done.79, s32[1024]{0:T(1024)S(1)} %copy-done.63, s32[1024]{0:T(1024)S(1)} %copy-done.65, s32[]{:T(128)S(6)} %select_n.333, s32[1024]{0:T(1024)S(1)} %copy-done.69, s32[1024]{0:T(1024)S(1)} %copy-done.67, ...), kind=kOutput, calls=%fused_computation.139 | convolution fusion | flops 1915551744 | bytes 7573516 | tf_op jit(solution)/shard_map/dot_general | solution.py:40
  215.1 6.4 %multiply_reduce_fusion = (f32[256]{0:T(256)S(1)}, f32[256,960]{0,1:T(8,128)}) fusion(f32[256,960]{0,1:T(8,128)} %copy-done.20, f32[256]{0:T(256)S(1)} %add_rsqrt_fusion, f32[256,960]{0,1:T(8,128)} %fusion.65, pred[960,1024]{1,0:T(32,128)(4,1)} %copy-done.34, bf16[256,2560]{1,0:T(8,128)(2,1)S(1)} %get-tuple-element.36, bf16[1024,2560]{1,0:T(8,128)(2,1)} %copy-done.78), kind=kOutput, calls=%fused_computation.134 | convolution fusion | flops 1846738688 | bytes 10487808 | tf_op jit(solution)/shard_map/dot_general | solution.py:40
  231.3 7.7 %fusion.52 = f32[256,5,64]{0,2,1:T(8,128)} fusion(f32[5,256,256,3]{2,1,3,0:T(8,128)} %fusion.183, bf16[256,5,3,32]{0,3,2,1:T(8,128)(2,1)} %bitcast.253, bf16[256,5,3,32]{0,3,2,1:T(8,128)(2,1)S(1)} %bitcast.251, f32[5,3,256,256]{2,3,1,0:T(8,128)} %get-tuple-element.150, f32[5,3,256]{2,1,0:T(4,128)S(1)} %copy-done.97), kind=kOutput, calls=%fused_computation.124 | convolution fusion | flops 133697536 | bytes 8698880 | tf_op jit(solution)/shard_map/kgqt,qkgd->tkd/dot_general | solution.py:163
  238.9 7.8 %fusion.43 = f32[5,64,3,256]{3,1,2,0:T(8,128)} fusion(f32[5,256,256,3]{2,1,3,0:T(8,128)} %fusion.183, bf16[256,5,32]{0,2,1:T(8,128)(2,1)S(1)} %copy-done.59, bf16[256,5,32]{0,2,1:T(8,128)(2,1)S(1)} %get-tuple-element.91, f32[5,3,256,256]{2,3,1,0:T(8,128)} %get-tuple-element.150, f32[5,3,256]{2,1,0:T(4,128)S(1)} %copy-done.97), kind=kOutput, calls=%fused_computation.92 | convolution fusion | flops 133042176 | bytes 9026560 | tf_op jit(solution)/shard_map/kgqt,tkd->qkgd/dot_general | solution.py:163
  297.9 6.7 %collective-permute-start.45 = (bf16[128,1280]{0,1:T(8,128)(2,1)S(1)}, bf16[128,1280]{0,1:T(8,128)(2,1)S(1)}, u32[]{:S(2)}, u32[]{:S(2)}) collective-permute-start(bf16[128,1280]{0,1:T(8,128)(2,1)S(1)} %get-tuple-element.59), channel_id=1, source_target_pairs={{0,12},{1,13},{2,14},{3,15},{4,0},{5,1},{6,2},{7,3},{8,4},{9,5},{1... | collective-permute-start | bytes 983048 | tf_op jit(solution)/shard_map/ppermute | solution.py:32
  306.4 6.5 %collective-permute-done.98 = bf16[4,80,448]{2,1,0:T(8,128)(2,1)S(1)} collective-permute-done((bf16[4,80,448]{2,1,0:T(8,128)(2,1)S(1)}, bf16[4,80,448]{2,1,0:T(8,128)(2,1)S(1)}, u32[]{:S(2)}, u32[]{:S(2)}) %collective-permute-start.98) | collective-permute-done | bytes 286752 | tf_op jit(solution)/shard_map/ppermute | solution.py:32
  313.1 6.6 %collective-permute-start.103 = (bf16[80,448]{1,0:T(8,128)(2,1)S(1)}, bf16[80,448]{1,0:T(8,128)(2,1)S(1)}, u32[]{:S(2)}, u32[]{:S(2)}) collective-permute-start(bf16[80,448]{1,0:T(8,128)(2,1)S(1)} %get-tuple-element.101), channel_id=1, source_target_pairs={{0,12},{1,13},{2,14},{3,15},{4,0},{5,1},{6,2},{7,3},{8,4},{9,5},{1... | collective-permute-start | bytes 215048 | tf_op jit(solution)/shard_map/ppermute | solution.py:32
  340.3 6.9 %collective-permute-done.56 = bf16[128,1280]{0,1:T(8,128)(2,1)S(1)} collective-permute-done((bf16[128,1280]{0,1:T(8,128)(2,1)S(1)}, bf16[128,1280]{0,1:T(8,128)(2,1)S(1)}, u32[]{:S(2)}, u32[]{:S(2)}) %collective-permute-start.56) | collective-permute-done | bytes 327712 | tf_op jit(solution)/shard_map/ppermute | solution.py:32
  351.0 5.7 %collective-permute-done.54 = bf16[128,1280]{0,1:T(8,128)(2,1)S(1)} collective-permute-done((bf16[128,1280]{0,1:T(8,128)(2,1)S(1)}, bf16[128,1280]{0,1:T(8,128)(2,1)S(1)}, u32[]{:S(2)}, u32[]{:S(2)}) %collective-permute-start.54) | collective-permute-done | bytes 327712 | tf_op jit(solution)/shard_map/ppermute | solution.py:32
  366.7 5.3 collective-permute-start.47
  381.8 5.0 collective-permute-done.46
  390.8 10.7 %collective-permute-start.91 = (bf16[80,512]{1,0:T(8,128)(2,1)S(1)}, bf16[80,512]{1,0:T(8,128)(2,1)S(1)}, u32[]{:S(2)}, u32[]{:S(2)}) collective-permute-start(bf16[80,512]{1,0:T(8,128)(2,1)S(1)} %get-tuple-element.99), channel_id=1, source_target_pairs={{0,2},{1,3},{2,0},{3,1},{4,6},{5,7},{6,4},{7,5},{8,10},{9,11},{10,... | collective-permute-start | bytes 245768 | tf_op jit(solution)/shard_map/ppermute | solution.py:32
  404.3 6.3 %collective-permute-start.50 = (bf16[32,1280]{0,1:T(8,128)(2,1)S(1)}, bf16[32,1280]{0,1:T(8,128)(2,1)S(1)}, u32[]{:S(2)}, u32[]{:S(2)}) collective-permute-start(bf16[32,1280]{0,1:T(8,128)(2,1)S(1)} %add_convert_fusion.9), channel_id=1, source_target_pairs={{0,32},{1,33},{2,34},{3,35},{4,36},{5,37},{6,38},{7,39},{8,40},{9,... | collective-permute-start | bytes 245768 | tf_op jit(solution)/shard_map/ppermute | solution.py:32
  413.1 9.9 %collective-permute-done.50 = bf16[32,1280]{0,1:T(8,128)(2,1)S(1)} collective-permute-done((bf16[32,1280]{0,1:T(8,128)(2,1)S(1)}, bf16[32,1280]{0,1:T(8,128)(2,1)S(1)}, u32[]{:S(2)}, u32[]{:S(2)}) %collective-permute-start.50) | collective-permute-done | bytes 81952 | tf_op jit(solution)/shard_map/ppermute | solution.py:32
  436.7 8.1 %collective-permute-start.52 = (bf16[32,1280]{0,1:T(8,128)(2,1)S(1)}, bf16[32,1280]{0,1:T(8,128)(2,1)S(1)}, u32[]{:S(2)}, u32[]{:S(2)}) collective-permute-start(bf16[32,1280]{0,1:T(8,128)(2,1)S(1)} %add_convert_fusion.8), channel_id=1, source_target_pairs={{0,16},{1,17},{2,18},{3,19},{4,20},{5,21},{6,22},{7,23},{8,24},{9,... | collective-permute-start | bytes 245768 | tf_op jit(solution)/shard_map/ppermute | solution.py:32
  469.8 8.4 %collective-permute-done.67 = bf16[128,2560]{1,0:T(8,128)(2,1)S(1)} collective-permute-done((bf16[128,2560]{1,0:T(8,128)(2,1)S(1)}, bf16[128,2560]{1,0:T(8,128)(2,1)S(1)}, u32[]{:S(2)}, u32[]{:S(2)}) %collective-permute-start.67) | collective-permute-done | bytes 655392 | tf_op jit(solution)/shard_map/ppermute | solution.py:32
  478.2 14.7 %collective-permute-done.66 = bf16[128,2560]{1,0:T(8,128)(2,1)S(1)} collective-permute-done((bf16[128,2560]{1,0:T(8,128)(2,1)S(1)}, bf16[128,2560]{1,0:T(8,128)(2,1)S(1)}, u32[]{:S(2)}, u32[]{:S(2)}) %collective-permute-start.66) | collective-permute-done | bytes 655392 | tf_op jit(solution)/shard_map/ppermute | solution.py:32
  497.4 11.7 %collective-permute-done.76 = bf16[128,2560]{1,0:T(8,128)(2,1)S(1)} collective-permute-done((bf16[128,2560]{1,0:T(8,128)(2,1)S(1)}, bf16[128,2560]{1,0:T(8,128)(2,1)S(1)}, u32[]{:S(2)}, u32[]{:S(2)}) %collective-permute-start.76) | collective-permute-done | bytes 655392 | tf_op jit(solution)/shard_map/ppermute | solution.py:32
  523.6 5.7 %collective-permute-start.74 = (bf16[32,2560]{1,0:T(8,128)(2,1)S(1)}, bf16[32,2560]{1,0:T(8,128)(2,1)S(1)}, u32[]{:S(2)}, u32[]{:S(2)}) collective-permute-start(bf16[32,2560]{1,0:T(8,128)(2,1)S(1)} %add_convert_fusion.15), channel_id=1, source_target_pairs={{0,16},{1,17},{2,18},{3,19},{4,20},{5,21},{6,22},{7,23},{8,24},{9,... | collective-permute-start | bytes 491528 | tf_op jit(solution)/shard_map/ppermute | solution.py:32
  529.9 6.3 %collective-permute-start.85 = (bf16[32,2560]{1,0:T(8,128)(2,1)S(1)}, bf16[32,2560]{1,0:T(8,128)(2,1)S(1)}, u32[]{:S(2)}, u32[]{:S(2)}) collective-permute-start(bf16[32,2560]{1,0:T(8,128)(2,1)S(1)} %add_convert_fusion.13), channel_id=1, source_target_pairs={{0,16},{1,17},{2,18},{3,19},{4,20},{5,21},{6,22},{7,23},{8,24},{9,... | collective-permute-start | bytes 491528 | tf_op jit(solution)/shard_map/ppermute | solution.py:32
  (589 shorter events, 344.0 us)
Async XLA Ops:
  5.0 37.5 %collective-permute-start = (bf16[32,1280]{1,0:T(8,128)(2,1)S(1)}, bf16[32,1280]{1,0:T(8,128)(2,1)}, u32[]{:S(2)}, u32[]{:S(2)}) collective-permute-start(bf16[32,1280]{1,0:T(8,128)(2,1)S(1)} %get-tuple-element.35), channel_id=1, source_target_pairs={{0,12},{1,13},{2,14},{3,15},{4,0},{5,1},{6,2},{7,3},{8,4},{9,5},{1... | collective-permute-start | bytes 245768 | tf_op jit(solution)/shard_map/ppermute | solution.py:32
  5.0 39.8 %collective-permute-start.1 = (bf16[32,1280]{1,0:T(8,128)(2,1)S(1)}, bf16[32,1280]{1,0:T(8,128)(2,1)}, u32[]{:S(2)}, u32[]{:S(2)}) collective-permute-start(bf16[32,1280]{1,0:T(8,128)(2,1)S(1)} %get-tuple-element.35), channel_id=1, source_target_pairs={{0,8},{1,9},{2,10},{3,11},{4,12},{5,13},{6,14},{7,15},{8,0},{9,1},... | collective-permute-start | bytes 245768 | tf_op jit(solution)/shard_map/ppermute | solution.py:32
  7.8 38.9 %collective-permute-start.2 = (bf16[32,1280]{1,0:T(8,128)(2,1)S(1)}, bf16[32,1280]{1,0:T(8,128)(2,1)}, u32[]{:S(2)}, u32[]{:S(2)}) collective-permute-start(bf16[32,1280]{1,0:T(8,128)(2,1)S(1)} %get-tuple-element.35), channel_id=1, source_target_pairs={{0,4},{1,5},{2,6},{3,7},{4,8},{5,9},{6,10},{7,11},{8,12},{9,13},{1... | collective-permute-start | bytes 245768 | tf_op jit(solution)/shard_map/ppermute | solution.py:32
  74.4 44.8 %collective-permute-start.5 = (bf16[128,1280]{1,0:T(8,128)(2,1)}, bf16[128,1280]{1,0:T(8,128)(2,1)}, u32[]{:S(2)}, u32[]{:S(2)}) collective-permute-start(bf16[128,1280]{1,0:T(8,128)(2,1)} %pad_maximum_fusion.11), channel_id=1, source_target_pairs={{0,1},{1,2},{2,3},{3,0},{4,5},{5,6},{6,7},{7,4},{8,9},{9,10},{10,1... | collective-permute-start | bytes 983048 | tf_op jit(solution)/shard_map/ppermute | solution.py:32
  76.2 33.3 %collective-permute-start.11 = (bf16[128,1280]{0,1:T(8,128)(2,1)S(1)}, bf16[128,1280]{0,1:T(8,128)(2,1)S(1)}, u32[]{:S(2)}, u32[]{:S(2)}) collective-permute-start(bf16[128,1280]{0,1:T(8,128)(2,1)S(1)} %pad_maximum_fusion.12), channel_id=1, source_target_pairs={{0,8},{1,9},{2,10},{3,11},{4,12},{5,13},{6,14},{7,15},{8,0},{9,1},... | collective-permute-start | bytes 983048 | tf_op jit(solution)/shard_map/ppermute | solution.py:32
  91.5 21.6 %collective-permute-start.12 = (bf16[128,1280]{0,1:T(8,128)(2,1)S(1)}, bf16[128,1280]{0,1:T(8,128)(2,1)}, u32[]{:S(2)}, u32[]{:S(2)}) collective-permute-start(bf16[128,1280]{0,1:T(8,128)(2,1)S(1)} %pad_maximum_fusion.12), channel_id=1, source_target_pairs={{0,4},{1,5},{2,6},{3,7},{4,8},{5,9},{6,10},{7,11},{8,12},{9,13},{1... | collective-permute-start | bytes 983048 | tf_op jit(solution)/shard_map/ppermute | solution.py:32
  109.5 36.6 %collective-permute-start.19 = (bf16[128,2560]{1,0:T(8,128)(2,1)}, bf16[128,2560]{1,0:T(8,128)(2,1)}, u32[]{:S(2)}, u32[]{:S(2)}) collective-permute-start(bf16[128,2560]{1,0:T(8,128)(2,1)} %pad_maximum_fusion.3), channel_id=1, source_target_pairs={{0,4},{1,5},{2,6},{3,7},{4,8},{5,9},{6,10},{7,11},{8,12},{9,13},{1... | collective-permute-start | bytes 1966088 | tf_op jit(solution)/shard_map/ppermute | solution.py:32
  113.1 35.5 %collective-permute-start.24 = (bf16[128,2560]{1,0:T(8,128)(2,1)}, bf16[128,2560]{1,0:T(8,128)(2,1)}, u32[]{:S(2)}, u32[]{:S(2)}) collective-permute-start(bf16[128,2560]{1,0:T(8,128)(2,1)} %pad_maximum_fusion.4), channel_id=1, source_target_pairs={{0,3},{1,0},{2,1},{3,2},{4,7},{5,4},{6,5},{7,6},{8,11},{9,8},{10,9... | collective-permute-start | bytes 1966088 | tf_op jit(solution)/shard_map/ppermute | solution.py:32
  119.2 33.8 %collective-permute-start.25 = (bf16[128,2560]{1,0:T(8,128)(2,1)}, bf16[128,2560]{1,0:T(8,128)(2,1)S(1)}, u32[]{:S(2)}, u32[]{:S(2)}) collective-permute-start(bf16[128,2560]{1,0:T(8,128)(2,1)} %pad_maximum_fusion.4), channel_id=1, source_target_pairs={{0,2},{1,3},{2,0},{3,1},{4,6},{5,7},{6,4},{7,5},{8,10},{9,11},{10,... | collective-permute-start | bytes 1966088 | tf_op jit(solution)/shard_map/ppermute | solution.py:32
  121.2 33.0 %collective-permute-start.26 = (bf16[128,2560]{1,0:T(8,128)(2,1)}, bf16[128,2560]{1,0:T(8,128)(2,1)S(1)}, u32[]{:S(2)}, u32[]{:S(2)}) collective-permute-start(bf16[128,2560]{1,0:T(8,128)(2,1)} %pad_maximum_fusion.4), channel_id=1, source_target_pairs={{0,1},{1,2},{2,3},{3,0},{4,5},{5,6},{6,7},{7,4},{8,9},{9,10},{10,1... | collective-permute-start | bytes 1966088 | tf_op jit(solution)/shard_map/ppermute | solution.py:32
  127.9 31.5 %collective-permute-start.41 = (bf16[4,4,80,448]{3,2,1,0:T(8,128)(2,1)S(1)}, bf16[4,4,80,448]{3,2,1,0:T(8,128)(2,1)S(1)}, u32[]{:S(2)}, u32[]{:S(2)}) collective-permute-start(bf16[4,4,80,448]{3,2,1,0:T(8,128)(2,1)S(1)} %bitcast_dynamic-update-slice_fusion.3), channel_id=1, source_target_pairs={{0,16},{1,17},{2,18},{3,19},{4,20},{5,21},{6,22},{7,23},{8,24},{9,... | collective-permute-start | bytes 3440648 | tf_op jit(solution)/shard_map/ppermute | solution.py:32
  146.1 32.6 %collective-permute-start.6 = (bf16[512,1280]{1,0:T(8,128)(2,1)}, bf16[512,1280]{1,0:T(8,128)(2,1)}, u32[]{:S(2)}, u32[]{:S(2)}) collective-permute-start(bf16[512,1280]{1,0:T(8,128)(2,1)} %get-tuple-element.113), channel_id=1, source_target_pairs={{0,16},{1,17},{2,18},{3,19},{4,20},{5,21},{6,22},{7,23},{8,24},{9,... | collective-permute-start | bytes 3932168 | tf_op jit(solution)/shard_map/ppermute | solution.py:32
  153.0 34.5 %collective-permute-start.34 = (bf16[4,4,80,512]{3,2,1,0:T(8,128)(2,1)}, bf16[4,4,80,512]{3,2,1,0:T(8,128)(2,1)}, u32[]{:S(2)}, u32[]{:S(2)}) collective-permute-start(bf16[4,4,80,512]{3,2,1,0:T(8,128)(2,1)} %bitcast_dynamic-update-slice_fusion.4), channel_id=1, source_target_pairs={{0,16},{1,17},{2,18},{3,19},{4,20},{5,21},{6,22},{7,23},{8,24},{9,... | collective-permute-start | bytes 3932168 | tf_op jit(solution)/shard_map/ppermute | solution.py:32
  154.1 40.5 %collective-permute-start.20 = (bf16[512,2560]{1,0:T(8,128)(2,1)}, bf16[512,2560]{1,0:T(8,128)(2,1)}, u32[]{:S(2)}, u32[]{:S(2)}) collective-permute-start(bf16[512,2560]{1,0:T(8,128)(2,1)} %get-tuple-element.77), channel_id=1, source_target_pairs={{0,16},{1,17},{2,18},{3,19},{4,20},{5,21},{6,22},{7,23},{8,24},{9,... | collective-permute-start | bytes 7864328 | tf_op jit(solution)/shard_map/ppermute | solution.py:32
  159.4 39.0 %collective-permute-start.27 = (bf16[512,2560]{1,0:T(8,128)(2,1)}, bf16[512,2560]{1,0:T(8,128)(2,1)}, u32[]{:S(2)}, u32[]{:S(2)}) collective-permute-start(bf16[512,2560]{1,0:T(8,128)(2,1)} %get-tuple-element.83), channel_id=1, source_target_pairs={{0,16},{1,17},{2,18},{3,19},{4,20},{5,21},{6,22},{7,23},{8,24},{9,... | collective-permute-start | bytes 7864328 | tf_op jit(solution)/shard_map/ppermute | solution.py:32
  290.4 34.3 %collective-permute-start.86 = (bf16[4,4,80,512]{3,2,1,0:T(8,128)(2,1)S(1)}, bf16[4,4,80,512]{3,2,1,0:T(8,128)(2,1)S(1)}, u32[]{:S(2)}, u32[]{:S(2)}) collective-permute-start(bf16[4,4,80,512]{3,2,1,0:T(8,128)(2,1)S(1)} %dynamic-slice_bitcast_fusion.1), channel_id=1, source_target_pairs={{0,16},{1,17},{2,18},{3,19},{4,20},{5,21},{6,22},{7,23},{8,24},{9,... | collective-permute-start | bytes 3932168 | tf_op jit(solution)/shard_map/ppermute | solution.py:32
  297.9 39.8 %collective-permute-start.45 = (bf16[128,1280]{0,1:T(8,128)(2,1)S(1)}, bf16[128,1280]{0,1:T(8,128)(2,1)S(1)}, u32[]{:S(2)}, u32[]{:S(2)}) collective-permute-start(bf16[128,1280]{0,1:T(8,128)(2,1)S(1)} %get-tuple-element.59), channel_id=1, source_target_pairs={{0,12},{1,13},{2,14},{3,15},{4,0},{5,1},{6,2},{7,3},{8,4},{9,5},{1... | collective-permute-start | bytes 983048 | tf_op jit(solution)/shard_map/ppermute | solution.py:32
  331.1 127.7 %collective-permute-start.64 = (bf16[512,2560]{1,0:T(8,128)(2,1)}, bf16[512,2560]{1,0:T(8,128)(2,1)}, u32[]{:S(2)}, u32[]{:S(2)}) collective-permute-start(bf16[512,2560]{1,0:T(8,128)(2,1)} %convolution_convert_fusion.2), channel_id=1, source_target_pairs={{0,16},{1,17},{2,18},{3,19},{4,20},{5,21},{6,22},{7,23},{8,24},{9,... | collective-permute-start | bytes 7864328 | tf_op jit(solution)/shard_map/ppermute | solution.py:32
  335.0 128.9 %collective-permute-start.75 = (bf16[512,2560]{1,0:T(8,128)(2,1)}, bf16[512,2560]{1,0:T(8,128)(2,1)}, u32[]{:S(2)}, u32[]{:S(2)}) collective-permute-start(bf16[512,2560]{1,0:T(8,128)(2,1)} %convolution_convert_fusion.1), channel_id=1, source_target_pairs={{0,16},{1,17},{2,18},{3,19},{4,20},{5,21},{6,22},{7,23},{8,24},{9,... | collective-permute-start | bytes 7864328 | tf_op jit(solution)/shard_map/ppermute | solution.py:32
  461.9 31.0 %collective-permute-start.66 = (bf16[128,2560]{1,0:T(8,128)(2,1)S(1)}, bf16[128,2560]{1,0:T(8,128)(2,1)S(1)}, u32[]{:S(2)}, u32[]{:S(2)}) collective-permute-start(bf16[128,2560]{1,0:T(8,128)(2,1)S(1)} %get-tuple-element.44), channel_id=1, source_target_pairs={{0,8},{1,9},{2,10},{3,11},{4,12},{5,13},{6,14},{7,15},{8,0},{9,1},... | collective-permute-start | bytes 1966088 | tf_op jit(solution)/shard_map/ppermute | solution.py:32
  464.0 29.8 %collective-permute-start.65 = (bf16[128,2560]{1,0:T(8,128)(2,1)S(1)}, bf16[128,2560]{1,0:T(8,128)(2,1)S(1)}, u32[]{:S(2)}, u32[]{:S(2)}) collective-permute-start(bf16[128,2560]{1,0:T(8,128)(2,1)S(1)} %get-tuple-element.42), channel_id=1, source_target_pairs={{0,4},{1,5},{2,6},{3,7},{4,8},{5,9},{6,10},{7,11},{8,12},{9,13},{1... | collective-permute-start | bytes 1966088 | tf_op jit(solution)/shard_map/ppermute | solution.py:32
  466.7 30.0 %collective-permute-start.78 = (bf16[128,2560]{1,0:T(8,128)(2,1)S(1)}, bf16[128,2560]{1,0:T(8,128)(2,1)S(1)}, u32[]{:S(2)}, u32[]{:S(2)}) collective-permute-start(bf16[128,2560]{1,0:T(8,128)(2,1)S(1)} %get-tuple-element.40), channel_id=1, source_target_pairs={{0,3},{1,0},{2,1},{3,2},{4,7},{5,4},{6,5},{7,6},{8,11},{9,8},{10,9... | collective-permute-start | bytes 1966088 | tf_op jit(solution)/shard_map/ppermute | solution.py:32
  469.7 27.7 %collective-permute-start.77 = (bf16[128,2560]{1,0:T(8,128)(2,1)S(1)}, bf16[128,2560]{1,0:T(8,128)(2,1)S(1)}, u32[]{:S(2)}, u32[]{:S(2)}) collective-permute-start(bf16[128,2560]{1,0:T(8,128)(2,1)S(1)} %get-tuple-element.41), channel_id=1, source_target_pairs={{0,2},{1,3},{2,0},{3,1},{4,6},{5,7},{6,4},{7,5},{8,10},{9,11},{10,... | collective-permute-start | bytes 1966088 | tf_op jit(solution)/shard_map/ppermute | solution.py:32
  478.2 30.9 %collective-permute-start.76 = (bf16[128,2560]{1,0:T(8,128)(2,1)S(1)}, bf16[128,2560]{1,0:T(8,128)(2,1)S(1)}, u32[]{:S(2)}, u32[]{:S(2)}) collective-permute-start(bf16[128,2560]{1,0:T(8,128)(2,1)S(1)} %get-tuple-element.39), channel_id=1, source_target_pairs={{0,1},{1,2},{2,3},{3,0},{4,5},{5,6},{6,7},{7,4},{8,9},{9,10},{10,1... | collective-permute-start | bytes 1966088 | tf_op jit(solution)/shard_map/ppermute | solution.py:32
  (186 other events, 2001.7 us)
